TPU v7x, 32 devices: a whole 2x2x4 slice. The times are simulated.
32 devices in a mesh: set: 8 (over z, core), col: 4 (over y, x).
Axes of the slice: x: 2, y: 2, z: 4, core: 2. Of those that a mesh axis runs over, the one named last changes fastest.
Arguments:
- factor: float32 [8, 2, 131072], P('col'), may hold values from -8 to 8
- velocity: float32 [8, 2, 131072], P(None, None, ('set', 'col')), may hold values from -4 to 4
- labels: int32 [8, 17], P('set'), may hold values from 0 to 2
- counts: int32 [8, 131072], P('set'), may hold values from 1 to 28, as said below
Outputs:
- new_factor: float32 [8, 2, 131072], P(None, None, ('set', 'col'))
- new_velocity: float32 [8, 2, 131072], P(None, None, ('set', 'col'))
Inputs may be any that keep to these rules, and one draw needn't show every extreme that they name: `labels`: 0 selects the X basis, 1 the Y basis, 2 the Z basis. The counts of setting s lie between 1 and 4 + (24 s) // 7.
All inputs are finite; a program needn't handle non-finite values.
Results may differ from a plain program's by a relative error of at most 0.0003.
Values sent between devices are 32-bit elements; how exact they have to be, the bound alone decides.
A program may use at most 64 MiB of HBM per device.

v0:
```python
import functools

import jax
import jax.numpy as jnp
from jax import lax
from jax.experimental import pallas as pl
from jax.experimental.pallas import tpu as pltpu
from jax.sharding import PartitionSpec as P

QA = 8
QB = 9
LANES = 128

mixing = 0.1
penalty = 8.0
momentum = 0.9
step_size = 0.5
count_norm = 8.0
MESH = pl.DeviceIdType.MESH


def fold_parity(x):
    x = x ^ (x >> 8)
    x = x ^ (x >> 4)
    x = x ^ (x >> 2)
    x = x ^ (x >> 1)
    return x & 1


def bit_count(x):
    x = x - ((x >> 1) & 0x55555)
    x = (x & 0x33333) + ((x >> 2) & 0x33333)
    x = (x + (x >> 4)) & 0xF0F0F
    return (x + (x >> 8) + (x >> 16)) & 0xFF


def sign_matrix(mask, size):
    row = lax.broadcasted_iota(jnp.int32, (size, size), 0)
    col = lax.broadcasted_iota(jnp.int32, (size, size), 1)
    sign = 1 - 2 * fold_parity(row & col & mask)
    keep = ((row ^ col) & (mask ^ (size - 1))) == 0
    return jnp.where(keep, sign, 0).astype(jnp.float32).astype(jnp.bfloat16)


def split(x):
    high = x.astype(jnp.bfloat16)
    return high, (x - high.astype(jnp.float32)).astype(jnp.bfloat16)


def dot(a, b):
    return jnp.dot(a, b, preferred_element_type=jnp.float32)


def kernel(n_set, n_col, labels, factor, velocity, counts, out_factor, out_velocity,
           hb, high, low, g, y, psend, precv, wown, wrecv, fb, sw, ab, stat, stat_col, stat_sum, stat_all,
           xbuf, right_buf, left_buf,
           f_send, f_recv, p_send, p_recv, w_send, w_recv, c_send, c_recv, s_send, s_recv,
           x_send, x_recv, r_send, r_recv, l_send, l_recv, a_send, a_recv):
    rank = factor.shape[0]
    left, rsize = 2**QA, 2**QB
    order = left * rsize
    tiles = rsize // LANES
    total = n_col * rank
    chunk = left // n_col
    block = factor.shape[1] // n_set
    part = block // n_col
    zs = n_set // 2
    i = lax.axis_index("set")
    j = lax.axis_index("col")
    z, core = i // 2, i % 2

    def col_peer(s):
        return lax.rem(j + s, n_col)

    def set_peer(s):
        return lax.rem(i + s, n_set)

    def rows_of(index, size):
        return pl.ds(pl.multiple_of(index * size, size), size)

    barrier = pltpu.get_barrier_semaphore()
    for s in range(1, n_col):
        pl.semaphore_signal(barrier, inc=1, device_id=(i, col_peer(s)), device_id_type=MESH)
    for s in range(1, n_set):
        pl.semaphore_signal(barrier, inc=1, device_id=(set_peer(s), j), device_id_type=MESH)
    pl.semaphore_wait(barrier, n_col - 1 + n_set - 1)

    def copy(src, dst, send, recv, where):
        return pltpu.make_async_remote_copy(
            src_ref=src, dst_ref=dst, send_sem=send, recv_sem=recv, device_id=where, device_id_type=MESH)

    mine = pl.ds(j * rank, rank)
    f_copies = []
    for s in range(1, n_col):
        peer = col_peer(s)
        f_copies.append(copy(factor.at[:, rows_of(i * n_col + peer, part)], fb.at[mine],
                             f_send.at[s], f_recv.at[s], (i, peer)))
        f_copies[-1].start()

    nonz = jnp.int32(0)
    ymask = jnp.int32(0)
    scale = jnp.float32(1.0)
    for q in range(QA + QB):
        label = labels[0, q]
        bit = 1 << (QA + QB - 1 - q)
        nonz = nonz + jnp.where(label == 2, 0, bit)
        ymask = ymask + jnp.where(label == 1, bit, 0)
        scale = scale * jnp.where(label == 2, 1.0, 0.5).astype(jnp.float32)
    ha = sign_matrix(nonz >> QB, left)
    hb[...] = sign_matrix(nonz & (rsize - 1), rsize)

    index = (lax.broadcasted_iota(jnp.int32, (left, LANES), 0) * rsize
             + lax.broadcasted_iota(jnp.int32, (left, LANES), 1))

    def phases(b):
        phase = bit_count((index + b * LANES) & ymask) & 3
        odd = (phase & 1) == 1
        late = (1 - 2 * (phase >> 1)).astype(jnp.float32)
        mid = (1 - 2 * ((phase ^ (phase >> 1)) & 1)).astype(jnp.float32)
        return odd, late, mid

    square = jnp.zeros((left, LANES), jnp.float32)
    for b in range(tiles):
        odd, late, mid = phases(b)
        lanes = slice(b * LANES, (b + 1) * LANES)
        for r in range(rank):
            re = factor[r, pl.ds(2 * b, left, stride=2 * tiles), :]
            im = factor[r, pl.ds(2 * b + 1, left, stride=2 * tiles), :]
            square = square + re * re + im * im
            for c, x in enumerate((jnp.where(odd, im, re) * late, jnp.where(odd, re, im) * mid)):
                xh, xl = split(x)
                high[2 * r + c, :, lanes] = xh
                low[2 * r + c, :, lanes] = xl
    for rc in range(2 * rank):
        first = dot(ha, high[rc]) + dot(ha, low[rc])
        xh, xl = split(first)
        high[rc] = xh
        low[rc] = xl
    trace_part = jnp.sum(jnp.sum(square, axis=0, keepdims=True), axis=1, keepdims=True)

    p_copies = []
    for s in list(range(1, n_col)) + [0]:
        peer = col_peer(s)
        rows = rows_of(peer, chunk)
        xh = high[:, rows, :].reshape(2 * rank * chunk, rsize)
        xl = low[:, rows, :].reshape(2 * rank * chunk, rsize)
        second = (dot(xh, hb[...]) + dot(xl, hb[...])).reshape(2 * rank, chunk, rsize)
        g[:, rows, :] = second
        psend[s, :chunk, :] = scale * jnp.sum(second * second, axis=0)
        psend[s, chunk:, :] = jnp.broadcast_to(trace_part, (8, rsize))
        if s:
            p_copies.append(copy(psend.at[s], precv.at[s], p_send.at[s], p_recv.at[s], (i, peer)))
            p_copies[-1].start()

    for r in range(rank):
        fb[j * rank + r] = factor[r, rows_of(i * n_col + j, part), :]
    for c in f_copies:
        c.wait()
    every = fb[...].reshape(total * part, LANES)
    parity = lax.broadcasted_iota(jnp.int32, every.shape, 0) & 1
    swapped = jnp.where(parity == 0, pltpu.roll(every, total * part - 1, 0), -pltpu.roll(every, 1, 0))
    sw[...] = swapped.reshape(total, part, LANES)
    lane = lax.broadcasted_iota(jnp.int32, (total, LANES), 1)
    gram = jnp.zeros((total, LANES), jnp.float32)
    for b in range(total):
        real = jnp.sum(jnp.sum(fb[...] * fb[b][None], axis=1), axis=1, keepdims=True)
        imag = jnp.sum(jnp.sum(fb[...] * sw[b][None], axis=1), axis=1, keepdims=True)
        gram = jnp.where(lane == b, real, gram)
        gram = jnp.where(lane == LANES // 2 + b, imag, gram)
    stat[8:, :] = gram

    prob = psend[0]
    for s, c in enumerate(p_copies, 1):
        c.wait()
        prob = prob + precv[s]
    trace_value = prob[chunk : chunk + 1, :1]
    prob = prob[:chunk]
    quasi = (1.0 - mixing) * prob / trace_value + mixing / order
    count = jnp.concatenate(
        [counts[pl.ds(j * (chunk * tiles) + b, chunk, stride=tiles), :] for b in range(tiles)], axis=1
    ).astype(jnp.float32)
    weight = count / (count_norm * order * quasi)
    wown[...] = weight
    ratio = jnp.sum((weight * prob / trace_value).reshape(chunk // 8, 8, rsize), axis=0)
    folded = ratio[:, :LANES]
    for b in range(1, tiles):
        folded = folded + ratio[:, b * LANES : (b + 1) * LANES]
    stat[:8, :] = folded
    w_copies, c_copies = [], []
    for s in range(1, n_col):
        where = (i, col_peer(s))
        w_copies.append(copy(wown, wrecv.at[s], w_send.at[s], w_recv.at[s], where))
        w_copies[-1].start()
        c_copies.append(copy(stat, stat_col.at[s], c_send.at[s], c_recv.at[s], where))
        c_copies[-1].start()

    for s in range(n_col):
        if s:
            w_copies[s - 1].wait()
            weight = wrecv[s]
        else:
            weight = wown[...]
        rows = rows_of(lax.rem(j - s + n_col, n_col), chunk)
        xh, xl = split((g[:, rows, :] * (weight * scale)[None]).reshape(2 * rank * chunk, rsize))
        xh, xl = split(dot(xh, hb[...]) + dot(xl, hb[...]))
        high[:, rows, :] = xh.reshape(2 * rank, chunk, rsize)
        low[:, rows, :] = xl.reshape(2 * rank, chunk, rsize)

    summed = stat[...]
    for s, c in enumerate(c_copies, 1):
        c.wait()
        summed = summed + stat_col[s]
    stat_sum[...] = summed
    s_copies = []
    for s in range(1, n_set):
        s_copies.append(copy(stat_sum, stat_all.at[s], s_send.at[s], s_recv.at[s], (set_peer(s), j)))
        s_copies[-1].start()

    odd_late_mid = [phases(b) for b in range(tiles)]
    for r in range(rank):
        re_all = dot(ha, high[2 * r]) + dot(ha, low[2 * r])
        im_all = dot(ha, high[2 * r + 1]) + dot(ha, low[2 * r + 1])
        for b in range(tiles):
            odd, late, mid = odd_late_mid[b]
            re = re_all[:, b * LANES : (b + 1) * LANES]
            im = im_all[:, b * LANES : (b + 1) * LANES]
            y[r, pl.ds(2 * b, left, stride=2 * tiles), :] = jnp.where(odd, im, re) * mid
            y[r, pl.ds(2 * b + 1, left, stride=2 * tiles), :] = jnp.where(odd, re, im) * late

    def rows_for(d, side):
        return rows_of(2 * d + side, block)

    def across(r, d):
        return copy(y.at[r, rows_for(d, 1 - core)], xbuf.at[d, r], x_send.at[d, r], x_recv.at[d, r],
                    (2 * z + 1 - core, j))

    def rightward(r, d):
        return copy(y.at[r, rows_for(d, core)], right_buf.at[d, r], r_send.at[d, r], r_recv.at[d, r],
                    (lax.rem(i + 2, n_set), j))

    def leftward(r, d):
        return copy(y.at[r, rows_for(d, core)], left_buf.at[d, r], l_send.at[d, r], l_recv.at[d, r],
                    (lax.rem(i + n_set - 2, n_set), j))

    for t in range(zs):
        for r in range(rank):
            across(r, lax.rem(z + t + 1, zs)).start()
    for t in range(zs - 1):
        for r in range(rank):
            @pl.when(t >= z)
            def _():
                d = z + zs - 1 - t
                across(r, d).wait_recv()
                y[r, rows_for(d, core), :] += xbuf[d, r]

                @pl.when(z > 0)
                def _():
                    rightward(r, d).wait_recv()
                    y[r, rows_for(d, core), :] += right_buf[d, r]

                rightward(r, d).start()

            @pl.when(t >= zs - 1 - z)
            def _():
                d = t - (zs - 1 - z)
                across(r, d).wait_recv()
                y[r, rows_for(d, core), :] += xbuf[d, r]

                @pl.when(z < zs - 1)
                def _():
                    leftward(r, d).wait_recv()
                    y[r, rows_for(d, core), :] += left_buf[d, r]

                leftward(r, d).start()

    summed = stat_sum[...]
    for s, c in enumerate(s_copies, 1):
        c.wait()
        summed = summed + stat_all[s]
    ratio_total = jnp.sum(jnp.sum(summed[:8], axis=0, keepdims=True), axis=1, keepdims=True)
    gram = summed[8:]
    purity = jnp.sum(jnp.sum(gram * gram, axis=0, keepdims=True), axis=1, keepdims=True) / (trace_value * trace_value)
    settings_all = n_set * labels.shape[0]
    rate = (1.0 - mixing) / settings_all
    own = rate * ratio_total - 2.0 * penalty * purity
    for b in range(total):
        mixed = own * fb[b]
        for a in range(total):
            mixed = mixed + (2.0 * penalty / trace_value) * (
                gram[a : a + 1, b : b + 1] * fb[a]
                - gram[a : a + 1, LANES // 2 + b : LANES // 2 + b + 1] * sw[a])
        out_velocity[b] = momentum * velocity[b] + mixed

    a_copies = []
    for r in range(rank):
        across(r, z).wait_recv()
        y[r, rows_for(z, core), :] += xbuf[z, r]

        @pl.when(z > 0)
        def _():
            rightward(r, z).wait_recv()
            y[r, rows_for(z, core), :] += right_buf[z, r]

        @pl.when(z < zs - 1)
        def _():
            leftward(r, z).wait_recv()
            y[r, rows_for(z, core), :] += left_buf[z, r]

        for s in range(1, n_col):
            peer = col_peer(s)
            a_copies.append(copy(y.at[r, rows_of(i * n_col + peer, part)], ab.at[j * rank + r],
                                 a_send.at[s, r], a_recv.at[s, r], (i, peer)))
            a_copies[-1].start()
        ab[j * rank + r] = y[r, rows_of(i * n_col + j, part), :]

    for t in range(zs):
        for r in range(rank):
            across(r, lax.rem(z + t + 1, zs)).wait_send()
    for t in range(zs - 1):
        for r in range(rank):
            @pl.when(t >= z)
            def _():
                rightward(r, z + zs - 1 - t).wait_send()

            @pl.when(t >= zs - 1 - z)
            def _():
                leftward(r, t - (zs - 1 - z)).wait_send()

    for c in a_copies:
        c.wait()
    new_velocity = out_velocity[...] - rate * ab[...]
    out_velocity[...] = new_velocity
    out_factor[...] = fb[...] - step_size * new_velocity


def interleave(x):
    n, two, m = x.shape
    return x.reshape(n, two, m // LANES, LANES).transpose(0, 2, 1, 3).reshape(n, two * m // LANES, LANES)


def separate(x):
    n, rows, lanes = x.shape
    return x.reshape(n, rows // 2, 2, lanes).transpose(0, 2, 1, 3).reshape(n, 2, rows // 2 * lanes)


def shards(n_set, n_col, factor, velocity, labels, counts):
    rank, _, order = factor.shape
    total = rank * n_col
    left, rsize = 2**QA, 2**QB
    chunk = left // n_col
    wide = 2 * order // LANES
    block = wide // n_set
    part = block // n_col
    zs = n_set // 2
    f32, bf16 = jnp.float32, jnp.bfloat16
    vmem = pl.BlockSpec(memory_space=pltpu.VMEM)
    dma = pltpu.SemaphoreType.DMA
    out = jax.ShapeDtypeStruct((total, part, LANES), f32)
    new_factor, new_velocity = pl.pallas_call(
        functools.partial(kernel, n_set, n_col),
        out_shape=(out, out),
        in_specs=[pl.BlockSpec(memory_space=pltpu.SMEM), vmem, vmem, vmem],
        out_specs=(vmem, vmem),
        scratch_shapes=[
            pltpu.VMEM((rsize, rsize), bf16),
            pltpu.VMEM((2 * rank, left, rsize), bf16),
            pltpu.VMEM((2 * rank, left, rsize), bf16),
            pltpu.VMEM((2 * rank, left, rsize), f32),
            pltpu.VMEM((rank, wide, LANES), f32),
            pltpu.VMEM((n_col, chunk + 8, rsize), f32),
            pltpu.VMEM((n_col, chunk + 8, rsize), f32),
            pltpu.VMEM((chunk, rsize), f32),
            pltpu.VMEM((n_col, chunk, rsize), f32),
            pltpu.VMEM((total, part, LANES), f32),
            pltpu.VMEM((total, part, LANES), f32),
            pltpu.VMEM((total, part, LANES), f32),
            pltpu.VMEM((8 + total, LANES), f32),
            pltpu.VMEM((n_col, 8 + total, LANES), f32),
            pltpu.VMEM((8 + total, LANES), f32),
            pltpu.VMEM((n_set, 8 + total, LANES), f32),
            pltpu.VMEM((zs, rank, block, LANES), f32),
            pltpu.VMEM((zs, rank, block, LANES), f32),
            pltpu.VMEM((zs, rank, block, LANES), f32),
            dma((n_col,)), dma((n_col,)), dma((n_col,)), dma((n_col,)), dma((n_col,)), dma((n_col,)),
            dma((n_col,)), dma((n_col,)), dma((n_set,)), dma((n_set,)),
            dma((zs, rank)), dma((zs, rank)), dma((zs, rank)), dma((zs, rank)), dma((zs, rank)), dma((zs, rank)),
            dma((n_col, rank)), dma((n_col, rank)),
        ],
        compiler_params=pltpu.CompilerParams(
            collective_id=0, has_side_effects=True, vmem_limit_bytes=48 * 2**20),
        name="tomography_step",
    )(labels, interleave(factor), interleave(velocity), counts.reshape(order // LANES, LANES))
    return separate(new_factor), separate(new_velocity)


def solution(mesh):
    in_specs = (P("col", None, None), P(None, None, ("set", "col")), P("set", None), P("set", None))
    out_specs = (P(None, None, ("set", "col")), P(None, None, ("set", "col")))
    body = functools.partial(shards, mesh.shape["set"], mesh.shape["col"])
    return jax.shard_map(body, mesh=mesh, in_specs=in_specs, out_specs=out_specs, check_vma=False)
```

profile of v0, /device:TPU:0, one launch (start us, length us, event | category | flops | bytes accessed | tf_op | source)
XLA Modules:
  0.0 57.6 jit_solution(11597137798285433608)
XLA Ops:
  0.6 0.0 copy-start
  0.6 1.6 %copy-done = f32[2,2,131072]{2,1,0:T(2,128)S(1)} copy-done((f32[2,2,131072]{2,1,0:T(2,128)S(1)}, f32[2,2,131072]{2,1,0:T(2,128)}, u32[]{:S(2)}) %copy-start) | copy-done | bytes 2097176
  2.2 0.0 copy-start.1
  2.2 1.0 %copy-done.1 = s32[1,131072]{1,0:T(1,128)S(1)} copy-done((s32[1,131072]{1,0:T(1,128)S(1)}, s32[1,131072]{1,0:T(1,128)}, u32[]{:S(2)}) %copy-start.1) | copy-done | bytes 524312
  3.3 0.0 copy-start.2
  3.3 0.9 %copy-done.2 = f32[8,2,4096]{2,1,0:T(2,128)S(1)} copy-done((f32[8,2,4096]{2,1,0:T(2,128)S(1)}, f32[8,2,4096]{2,1,0:T(2,128)}, u32[]{:S(2)}) %copy-start.2) | copy-done | bytes 262168
  4.2 0.0 copy-start.3
  4.2 0.7 %copy-done.3 = s32[1,17]{1,0:T(1,128)S(1)} copy-done((s32[1,17]{1,0:T(1,128)S(1)}, s32[1,17]{1,0:T(1,128)}, u32[]{:S(2)}) %copy-start.3) | copy-done | bytes 92
  4.9 51.3 %tomography_step.1 = (f32[8,64,128]{2,1,0:T(8,128)S(1)}, f32[8,64,128]{2,1,0:T(8,128)S(1)}) custom-call(s32[1,17]{1,0:T(1,128)S(1)} %copy-done.3, f32[2,2048,128]{2,1,0:T(8,128)S(1)} %bitcast.21, f32[8,64,128]{2,1,0:T(8,128)S(1)} %bitcast.23, s32[1024,128]{1,0:T(8,128)S(1)} %bitcast.22), custom_call_target="tpu_custom_call" | custom-call | tf_op jit(solution)/shard_map/tomography_step/pallas_call | solution.py:359
  56.2 0.7 %copy.12 = f32[8,2,4096]{2,1,0:T(2,128)} copy(f32[8,2,4096]{2,1,0:T(2,128)S(1)} %bitcast.25) | data formatting | bytes 524288
  56.9 0.7 %copy.13 = f32[8,2,4096]{2,1,0:T(2,128)} copy(f32[8,2,4096]{2,1,0:T(2,128)S(1)} %bitcast.24) | data formatting | bytes 524288
Async XLA Ops:
  0.6 1.6 %copy-start = (f32[2,2,131072]{2,1,0:T(2,128)S(1)}, f32[2,2,131072]{2,1,0:T(2,128)}, u32[]{:S(2)}) copy-start(f32[2,2,131072]{2,1,0:T(2,128)} %param.4) | copy-start | bytes 6291460
  2.2 1.0 %copy-start.1 = (s32[1,131072]{1,0:T(1,128)S(1)}, s32[1,131072]{1,0:T(1,128)}, u32[]{:S(2)}) copy-start(s32[1,131072]{1,0:T(1,128)} %param.7) | copy-start | bytes 1572868
  3.3 0.9 %copy-start.2 = (f32[8,2,4096]{2,1,0:T(2,128)S(1)}, f32[8,2,4096]{2,1,0:T(2,128)}, u32[]{:S(2)}) copy-start(f32[8,2,4096]{2,1,0:T(2,128)} %param.5) | copy-start | bytes 786436
  4.2 0.7 %copy-start.3 = (s32[1,17]{1,0:T(1,128)S(1)}, s32[1,17]{1,0:T(1,128)}, u32[]{:S(2)}) copy-start(s32[1,17]{1,0:T(1,128)} %labels.1) | copy-start | bytes 208
where the time goes:
time: 57.9 us; the launch traced here: 57.6 us
  Pallas kernels  51.3 us (89%)
  local copies, waits for them, and re-layouts  5.64 us (10%)
  between operations  0.65 us (1%)
    pallas_call x1, Pallas kernels, shards(): pl.pallas_call(functools.partial(kernel, n_set, n_col), out_shape=(out, o...  51.3 us
    unnamed x10, local copies, waits for them, and re-layouts  5.64 us

commit v1 on v0

--- a/solution.py
+++ b/solution.py
@@ -51,11 +51,11 @@
     return jnp.dot(a, b, preferred_element_type=jnp.float32)
 
 
-def kernel(n_set, n_col, labels, factor, velocity, counts, out_factor, out_velocity,
-           hb, high, low, g, y, psend, precv, wown, wrecv, fb, sw, ab, stat, stat_col, stat_sum, stat_all,
+def kernel(n_set, n_col, labels, factor_hbm, velocity_hbm, counts_hbm, out_factor, out_base, out_adjoint,
+           factor, velocity, counts, hb, high, low, g, y, psend, precv, wown, wrecv, fb, sw, ab, stat, stat_col, stat_sum, stat_all,
            xbuf, right_buf, left_buf,
            f_send, f_recv, p_send, p_recv, w_send, w_recv, c_send, c_recv, s_send, s_recv,
-           x_send, x_recv, r_send, r_recv, l_send, l_recv, a_send, a_recv):
+           x_send, x_recv, r_send, r_recv, l_send, l_recv, a_send, a_recv, load_sem):
     rank = factor.shape[0]
     left, rsize = 2**QA, 2**QB
     order = left * rsize
@@ -78,24 +78,20 @@
     def rows_of(index, size):
         return pl.ds(pl.multiple_of(index * size, size), size)
 
+    loads = [pltpu.make_async_copy(factor_hbm.at[r], factor.at[r], load_sem.at[r]) for r in range(rank)]
+    loads.append(pltpu.make_async_copy(counts_hbm, counts, load_sem.at[rank]))
+    loads.append(pltpu.make_async_copy(velocity_hbm, velocity, load_sem.at[rank + 1]))
+    for load in loads:
+        load.start()
     barrier = pltpu.get_barrier_semaphore()
     for s in range(1, n_col):
         pl.semaphore_signal(barrier, inc=1, device_id=(i, col_peer(s)), device_id_type=MESH)
     for s in range(1, n_set):
         pl.semaphore_signal(barrier, inc=1, device_id=(set_peer(s), j), device_id_type=MESH)
-    pl.semaphore_wait(barrier, n_col - 1 + n_set - 1)
 
     def copy(src, dst, send, recv, where):
         return pltpu.make_async_remote_copy(
             src_ref=src, dst_ref=dst, send_sem=send, recv_sem=recv, device_id=where, device_id_type=MESH)
-
-    mine = pl.ds(j * rank, rank)
-    f_copies = []
-    for s in range(1, n_col):
-        peer = col_peer(s)
-        f_copies.append(copy(factor.at[:, rows_of(i * n_col + peer, part)], fb.at[mine],
-                             f_send.at[s], f_recv.at[s], (i, peer)))
-        f_copies[-1].start()
 
     nonz = jnp.int32(0)
     ymask = jnp.int32(0)
@@ -119,6 +115,8 @@
         mid = (1 - 2 * ((phase ^ (phase >> 1)) & 1)).astype(jnp.float32)
         return odd, late, mid
 
+    for load in loads[:rank]:
+        load.wait()
     square = jnp.zeros((left, LANES), jnp.float32)
     for b in range(tiles):
         odd, late, mid = phases(b)
@@ -136,6 +134,7 @@
         xh, xl = split(first)
         high[rc] = xh
         low[rc] = xl
+    pl.semaphore_wait(barrier, n_col - 1 + n_set - 1)
     trace_part = jnp.sum(jnp.sum(square, axis=0, keepdims=True), axis=1, keepdims=True)
 
     p_copies = []
@@ -152,23 +151,6 @@
             p_copies.append(copy(psend.at[s], precv.at[s], p_send.at[s], p_recv.at[s], (i, peer)))
             p_copies[-1].start()
 
-    for r in range(rank):
-        fb[j * rank + r] = factor[r, rows_of(i * n_col + j, part), :]
-    for c in f_copies:
-        c.wait()
-    every = fb[...].reshape(total * part, LANES)
-    parity = lax.broadcasted_iota(jnp.int32, every.shape, 0) & 1
-    swapped = jnp.where(parity == 0, pltpu.roll(every, total * part - 1, 0), -pltpu.roll(every, 1, 0))
-    sw[...] = swapped.reshape(total, part, LANES)
-    lane = lax.broadcasted_iota(jnp.int32, (total, LANES), 1)
-    gram = jnp.zeros((total, LANES), jnp.float32)
-    for b in range(total):
-        real = jnp.sum(jnp.sum(fb[...] * fb[b][None], axis=1), axis=1, keepdims=True)
-        imag = jnp.sum(jnp.sum(fb[...] * sw[b][None], axis=1), axis=1, keepdims=True)
-        gram = jnp.where(lane == b, real, gram)
-        gram = jnp.where(lane == LANES // 2 + b, imag, gram)
-    stat[8:, :] = gram
-
     prob = psend[0]
     for s, c in enumerate(p_copies, 1):
         c.wait()
@@ -176,23 +158,29 @@
     trace_value = prob[chunk : chunk + 1, :1]
     prob = prob[:chunk]
     quasi = (1.0 - mixing) * prob / trace_value + mixing / order
+    loads[rank].wait()
     count = jnp.concatenate(
         [counts[pl.ds(j * (chunk * tiles) + b, chunk, stride=tiles), :] for b in range(tiles)], axis=1
     ).astype(jnp.float32)
     weight = count / (count_norm * order * quasi)
     wown[...] = weight
+    w_copies = []
+    for s in range(1, n_col):
+        w_copies.append(copy(wown, wrecv.at[s], w_send.at[s], w_recv.at[s], (i, col_peer(s))))
+        w_copies[-1].start()
     ratio = jnp.sum((weight * prob / trace_value).reshape(chunk // 8, 8, rsize), axis=0)
     folded = ratio[:, :LANES]
     for b in range(1, tiles):
         folded = folded + ratio[:, b * LANES : (b + 1) * LANES]
     stat[:8, :] = folded
-    w_copies, c_copies = [], []
+
+    mine = pl.ds(j * rank, rank)
+    f_copies = []
     for s in range(1, n_col):
-        where = (i, col_peer(s))
-        w_copies.append(copy(wown, wrecv.at[s], w_send.at[s], w_recv.at[s], where))
-        w_copies[-1].start()
-        c_copies.append(copy(stat, stat_col.at[s], c_send.at[s], c_recv.at[s], where))
-        c_copies[-1].start()
+        peer = col_peer(s)
+        f_copies.append(copy(factor.at[:, rows_of(i * n_col + peer, part)], fb.at[mine],
+                             f_send.at[s], f_recv.at[s], (i, peer)))
+        f_copies[-1].start()
 
     for s in range(n_col):
         if s:
@@ -206,15 +194,20 @@
         high[:, rows, :] = xh.reshape(2 * rank, chunk, rsize)
         low[:, rows, :] = xl.reshape(2 * rank, chunk, rsize)
 
-    summed = stat[...]
-    for s, c in enumerate(c_copies, 1):
-        c.wait()
-        summed = summed + stat_col[s]
-    stat_sum[...] = summed
-    s_copies = []
-    for s in range(1, n_set):
-        s_copies.append(copy(stat_sum, stat_all.at[s], s_send.at[s], s_recv.at[s], (set_peer(s), j)))
-        s_copies[-1].start()
+    def rows_for(d, side):
+        return rows_of(2 * d + side, block)
+
+    def across(r, d):
+        return copy(y.at[r, rows_for(d, 1 - core)], xbuf.at[d, r], x_send.at[d, r], x_recv.at[d, r],
+                    (2 * z + 1 - core, j))
+
+    def rightward(r, d):
+        return copy(y.at[r, rows_for(d, core)], right_buf.at[d, r], r_send.at[d, r], r_recv.at[d, r],
+                    (lax.rem(i + 2, n_set), j))
+
+    def leftward(r, d):
+        return copy(y.at[r, rows_for(d, core)], left_buf.at[d, r], l_send.at[d, r], l_recv.at[d, r],
+                    (lax.rem(i + n_set - 2, n_set), j))
 
     odd_late_mid = [phases(b) for b in range(tiles)]
     for r in range(rank):
@@ -226,25 +219,16 @@
             im = im_all[:, b * LANES : (b + 1) * LANES]
             y[r, pl.ds(2 * b, left, stride=2 * tiles), :] = jnp.where(odd, im, re) * mid
             y[r, pl.ds(2 * b + 1, left, stride=2 * tiles), :] = jnp.where(odd, re, im) * late
-
-    def rows_for(d, side):
-        return rows_of(2 * d + side, block)
-
-    def across(r, d):
-        return copy(y.at[r, rows_for(d, 1 - core)], xbuf.at[d, r], x_send.at[d, r], x_recv.at[d, r],
-                    (2 * z + 1 - core, j))
-
-    def rightward(r, d):
-        return copy(y.at[r, rows_for(d, core)], right_buf.at[d, r], r_send.at[d, r], r_recv.at[d, r],
-                    (lax.rem(i + 2, n_set), j))
-
-    def leftward(r, d):
-        return copy(y.at[r, rows_for(d, core)], left_buf.at[d, r], l_send.at[d, r], l_recv.at[d, r],
-                    (lax.rem(i + n_set - 2, n_set), j))
-
-    for t in range(zs):
-        for r in range(rank):
-            across(r, lax.rem(z + t + 1, zs)).start()
+        for t in range(zs - 1):
+            @pl.when(t >= z)
+            def _():
+                across(r, z + zs - 1 - t).start()
+
+            @pl.when(t >= zs - 1 - z)
+            def _():
+                across(r, t - (zs - 1 - z)).start()
+        across(r, z).start()
+
     for t in range(zs - 1):
         for r in range(rank):
             @pl.when(t >= z)
@@ -272,6 +256,38 @@
                     y[r, rows_for(d, core), :] += left_buf[d, r]
 
                 leftward(r, d).start()
+
+        if t == 0:
+            for r in range(rank):
+                fb[j * rank + r] = factor[r, rows_of(i * n_col + j, part), :]
+            for c in f_copies:
+                c.wait()
+            every = fb[...].reshape(total * part, LANES)
+            parity = lax.broadcasted_iota(jnp.int32, every.shape, 0) & 1
+            swapped = jnp.where(parity == 0, pltpu.roll(every, total * part - 1, 0), -pltpu.roll(every, 1, 0))
+            sw[...] = swapped.reshape(total, part, LANES)
+            lane = lax.broadcasted_iota(jnp.int32, (total, LANES), 1)
+            gram = jnp.zeros((total, LANES), jnp.float32)
+            for b in range(total):
+                real = jnp.sum(jnp.sum(fb[...] * fb[b][None], axis=1), axis=1, keepdims=True)
+                imag = jnp.sum(jnp.sum(fb[...] * sw[b][None], axis=1), axis=1, keepdims=True)
+                gram = jnp.where(lane == b, real, gram)
+                gram = jnp.where(lane == LANES // 2 + b, imag, gram)
+            stat[8:, :] = gram
+            c_copies = []
+            for s in range(1, n_col):
+                c_copies.append(copy(stat, stat_col.at[s], c_send.at[s], c_recv.at[s], (i, col_peer(s))))
+                c_copies[-1].start()
+        if t == min(1, zs - 2):
+            summed = stat[...]
+            for s, c in enumerate(c_copies, 1):
+                c.wait()
+                summed = summed + stat_col[s]
+            stat_sum[...] = summed
+            s_copies = []
+            for s in range(1, n_set):
+                s_copies.append(copy(stat_sum, stat_all.at[s], s_send.at[s], s_recv.at[s], (set_peer(s), j)))
+                s_copies[-1].start()
 
     summed = stat_sum[...]
     for s, c in enumerate(s_copies, 1):
@@ -283,13 +299,15 @@
     settings_all = n_set * labels.shape[0]
     rate = (1.0 - mixing) / settings_all
     own = rate * ratio_total - 2.0 * penalty * purity
+    loads[rank + 1].wait()
     for b in range(total):
         mixed = own * fb[b]
         for a in range(total):
             mixed = mixed + (2.0 * penalty / trace_value) * (
                 gram[a : a + 1, b : b + 1] * fb[a]
                 - gram[a : a + 1, LANES // 2 + b : LANES // 2 + b + 1] * sw[a])
-        out_velocity[b] = momentum * velocity[b] + mixed
+        out_base[b] = momentum * velocity[b] + mixed
+    out_factor[...] = fb[...]
 
     a_copies = []
     for r in range(rank):
@@ -328,9 +346,7 @@
 
     for c in a_copies:
         c.wait()
-    new_velocity = out_velocity[...] - rate * ab[...]
-    out_velocity[...] = new_velocity
-    out_factor[...] = fb[...] - step_size * new_velocity
+    out_adjoint[...] = rate * ab[...]
 
 
 def interleave(x):
@@ -354,14 +370,18 @@
     zs = n_set // 2
     f32, bf16 = jnp.float32, jnp.bfloat16
     vmem = pl.BlockSpec(memory_space=pltpu.VMEM)
+    hbm = pl.BlockSpec(memory_space=pltpu.HBM)
     dma = pltpu.SemaphoreType.DMA
     out = jax.ShapeDtypeStruct((total, part, LANES), f32)
-    new_factor, new_velocity = pl.pallas_call(
+    kept, base, adjoint = pl.pallas_call(
         functools.partial(kernel, n_set, n_col),
-        out_shape=(out, out),
-        in_specs=[pl.BlockSpec(memory_space=pltpu.SMEM), vmem, vmem, vmem],
-        out_specs=(vmem, vmem),
+        out_shape=(out, out, out),
+        in_specs=[pl.BlockSpec(memory_space=pltpu.SMEM), hbm, hbm, hbm],
+        out_specs=(vmem, vmem, vmem),
         scratch_shapes=[
+            pltpu.VMEM((rank, wide, LANES), f32),
+            pltpu.VMEM((total, part, LANES), f32),
+            pltpu.VMEM((order // LANES, LANES), jnp.int32),
             pltpu.VMEM((rsize, rsize), bf16),
             pltpu.VMEM((2 * rank, left, rsize), bf16),
             pltpu.VMEM((2 * rank, left, rsize), bf16),
@@ -384,13 +404,14 @@
             dma((n_col,)), dma((n_col,)), dma((n_col,)), dma((n_col,)), dma((n_col,)), dma((n_col,)),
             dma((n_col,)), dma((n_col,)), dma((n_set,)), dma((n_set,)),
             dma((zs, rank)), dma((zs, rank)), dma((zs, rank)), dma((zs, rank)), dma((zs, rank)), dma((zs, rank)),
-            dma((n_col, rank)), dma((n_col, rank)),
+            dma((n_col, rank)), dma((n_col, rank)), dma((rank + 2,)),
         ],
         compiler_params=pltpu.CompilerParams(
-            collective_id=0, has_side_effects=True, vmem_limit_bytes=48 * 2**20),
+            collective_id=0, has_side_effects=True, vmem_limit_bytes=60 * 2**20),
         name="tomography_step",
     )(labels, interleave(factor), interleave(velocity), counts.reshape(order // LANES, LANES))
-    return separate(new_factor), separate(new_velocity)
+    new_velocity = separate(base) - separate(adjoint)
+    return separate(kept) - step_size * new_velocity, new_velocity
 
 
 def solution(mesh):

time: 57.9 us -> 54.5 us (0.941)
  local copies, waits for them, and re-layouts: 5.64 us -> 0.01 us
  other arithmetic: 0 us -> 2.97 us
  Pallas kernels: 51.3 us -> 50.7 us
    unnamed x10 -> x2, local copies, waits for them, and re-layouts: 5.64 us -> 0.01 us
    sub x0 -> x2, other arithmetic: none -> 2.97 us  [the longest x1 1.91 us: shards(): return (separate(kept) - step_size * new_velocity, new_velocity)]
    pallas_call x1, Pallas kernels: 51.3 us -> 50.7 us  [shards(): pl.pallas_call(functools.partial(kernel, n_set, n_col), out_shape=(out, o...]
where the time goes in v1:
time: 54.5 us; the launch traced here: 54.3 us
  Pallas kernels  50.7 us (93%)
  other arithmetic  2.97 us (5%)
  between operations  0.65 us (1%)
    pallas_call x1, Pallas kernels, shards(): pl.pallas_call(functools.partial(kernel, n_set, n_col), out_shape=(out, o...  50.7 us
    sub x1, other arithmetic, shards(): return (separate(kept) - step_size * new_velocity, new_velocity)  1.91 us

profile of v1, /device:TPU:0, one launch (start us, length us, event | category | flops | bytes accessed | tf_op | source)
XLA Modules:
  0.0 54.3 jit_solution(15451609237505522869)
XLA Ops:
  0.6 50.7 %tomography_step.1 = (f32[8,64,128]{2,1,0:T(8,128)}, f32[8,64,128]{2,1,0:T(8,128)}, f32[8,64,128]{2,1,0:T(8,128)}) custom-call(s32[1,17]{1,0:T(1,128)} %labels.1, f32[2,2048,128]{2,1,0:T(8,128)} %bitcast.21, f32[8,64,128]{2,1,0:T(8,128)} %bitcast.25, s32[1024,128]{1,0:T(8,128)} %bitcast.24), custom_call_target="tpu_custom_call" | custom-call | tf_op jit(solution)/shard_map/tomography_step/pallas_call | solution.py:376
  51.3 1.1 %sub.15 = f32[8,64,128]{2,1,0:T(8,128)S(1)} subtract(f32[8,64,128]{2,1,0:T(8,128)} %get-tuple-element.6, f32[8,64,128]{2,1,0:T(8,128)} %get-tuple-element.7) | non-fusion elementwise | flops 65536 | bytes 786432 | tf_op jit(solution)/shard_map/sub | solution.py:413
  52.4 0.0 copy-start
  52.4 1.9 %multiply_subtract_fusion = f32[8,2,4096]{2,1,0:T(2,128)} fusion(f32[8,2,4096]{2,1,0:T(2,128)} %bitcast.26, f32[8,2,4096]{2,1,0:T(2,128)S(1)} %bitcast.22), kind=kLoop, calls=%fused_computation | loop fusion | flops 131072 | bytes 786432 | tf_op jit(solution)/shard_map/sub | solution.py:414
  54.3 0.0 copy-done
Async XLA Ops:
  52.4 1.9 %copy-start = (f32[8,64,128]{2,1,0:T(8,128)}, f32[8,64,128]{2,1,0:T(8,128)S(1)}, u32[]{:S(2)}) copy-start(f32[8,64,128]{2,1,0:T(8,128)S(1)} %sub.15) | copy-start | bytes 786436

commit v2 on v1

--- a/solution.py
+++ b/solution.py
@@ -51,7 +51,7 @@
     return jnp.dot(a, b, preferred_element_type=jnp.float32)
 
 
-def kernel(n_set, n_col, labels, factor_hbm, velocity_hbm, counts_hbm, out_factor, out_base, out_adjoint,
+def kernel(n_set, n_col, labels, factor_hbm, velocity_hbm, counts_hbm, out_factor, out_velocity,
            factor, velocity, counts, hb, high, low, g, y, psend, precv, wown, wrecv, fb, sw, ab, stat, stat_col, stat_sum, stat_all,
            xbuf, right_buf, left_buf,
            f_send, f_recv, p_send, p_recv, w_send, w_recv, c_send, c_recv, s_send, s_recv,
@@ -174,14 +174,6 @@
         folded = folded + ratio[:, b * LANES : (b + 1) * LANES]
     stat[:8, :] = folded
 
-    mine = pl.ds(j * rank, rank)
-    f_copies = []
-    for s in range(1, n_col):
-        peer = col_peer(s)
-        f_copies.append(copy(factor.at[:, rows_of(i * n_col + peer, part)], fb.at[mine],
-                             f_send.at[s], f_recv.at[s], (i, peer)))
-        f_copies[-1].start()
-
     for s in range(n_col):
         if s:
             w_copies[s - 1].wait()
@@ -193,6 +185,14 @@
         xh, xl = split(dot(xh, hb[...]) + dot(xl, hb[...]))
         high[:, rows, :] = xh.reshape(2 * rank, chunk, rsize)
         low[:, rows, :] = xl.reshape(2 * rank, chunk, rsize)
+
+    mine = pl.ds(j * rank, rank)
+    f_copies = []
+    for s in range(1, n_col):
+        peer = col_peer(s)
+        f_copies.append(copy(factor.at[:, rows_of(i * n_col + peer, part)], fb.at[mine],
+                             f_send.at[s], f_recv.at[s], (i, peer)))
+        f_copies[-1].start()
 
     def rows_for(d, side):
         return rows_of(2 * d + side, block)
@@ -242,6 +242,10 @@
                     rightward(r, d).wait_recv()
                     y[r, rows_for(d, core), :] += right_buf[d, r]
 
+                @pl.when(t > z)
+                def _():
+                    rightward(r, d + 1).wait_send()
+
                 rightward(r, d).start()
 
             @pl.when(t >= zs - 1 - z)
@@ -254,6 +258,10 @@
                 def _():
                     leftward(r, d).wait_recv()
                     y[r, rows_for(d, core), :] += left_buf[d, r]
+
+                @pl.when(t > zs - 1 - z)
+                def _():
+                    leftward(r, d - 1).wait_send()
 
                 leftward(r, d).start()
 
@@ -306,8 +314,7 @@
             mixed = mixed + (2.0 * penalty / trace_value) * (
                 gram[a : a + 1, b : b + 1] * fb[a]
                 - gram[a : a + 1, LANES // 2 + b : LANES // 2 + b + 1] * sw[a])
-        out_base[b] = momentum * velocity[b] + mixed
-    out_factor[...] = fb[...]
+        out_velocity[b] = momentum * velocity[b] + mixed
 
     a_copies = []
     for r in range(rank):
@@ -334,19 +341,20 @@
     for t in range(zs):
         for r in range(rank):
             across(r, lax.rem(z + t + 1, zs)).wait_send()
-    for t in range(zs - 1):
-        for r in range(rank):
-            @pl.when(t >= z)
-            def _():
-                rightward(r, z + zs - 1 - t).wait_send()
-
-            @pl.when(t >= zs - 1 - z)
-            def _():
-                leftward(r, t - (zs - 1 - z)).wait_send()
+    for r in range(rank):
+        @pl.when(z < zs - 1)
+        def _():
+            rightward(r, z + 1).wait_send()
+
+        @pl.when(z > 0)
+        def _():
+            leftward(r, z - 1).wait_send()
 
     for c in a_copies:
         c.wait()
-    out_adjoint[...] = rate * ab[...]
+    new_velocity = out_velocity[...] - rate * ab[...]
+    out_velocity[...] = new_velocity
+    out_factor[...] = fb[...] - step_size * new_velocity
 
 
 def interleave(x):
@@ -373,11 +381,11 @@
     hbm = pl.BlockSpec(memory_space=pltpu.HBM)
     dma = pltpu.SemaphoreType.DMA
     out = jax.ShapeDtypeStruct((total, part, LANES), f32)
-    kept, base, adjoint = pl.pallas_call(
+    new_factor, new_velocity = pl.pallas_call(
         functools.partial(kernel, n_set, n_col),
-        out_shape=(out, out, out),
+        out_shape=(out, out),
         in_specs=[pl.BlockSpec(memory_space=pltpu.SMEM), hbm, hbm, hbm],
-        out_specs=(vmem, vmem, vmem),
+        out_specs=(vmem, vmem),
         scratch_shapes=[
             pltpu.VMEM((rank, wide, LANES), f32),
             pltpu.VMEM((total, part, LANES), f32),
@@ -410,8 +418,7 @@
             collective_id=0, has_side_effects=True, vmem_limit_bytes=60 * 2**20),
         name="tomography_step",
     )(labels, interleave(factor), interleave(velocity), counts.reshape(order // LANES, LANES))
-    new_velocity = separate(base) - separate(adjoint)
-    return separate(kept) - step_size * new_velocity, new_velocity
+    return separate(new_factor), separate(new_velocity)
 
 
 def solution(mesh):

time: 54.5 us -> 53.6 us (0.983)
  local copies, waits for them, and re-layouts: 0.01 us -> 3.34 us
  other arithmetic: 2.97 us -> 0 us
  Pallas kernels: 50.7 us -> 49.4 us
    unnamed x2, local copies, waits for them, and re-layouts: 0.01 us -> 3.34 us
    sub x2 -> x0, other arithmetic: 2.97 us -> none  [the longest x1 1.91 us: shards(): return (separate(kept) - step_size * new_velocity, new_velocity)]
    pallas_call x1, Pallas kernels: 50.7 us -> 49.4 us  [shards(): pl.pallas_call(functools.partial(kernel, n_set, n_col), out_shape=(out, o...]
where the time goes in v2:
time: 53.6 us; the launch traced here: 53.4 us
  Pallas kernels  49.4 us (92%)
  local copies, waits for them, and re-layouts  3.34 us (6%)
  between operations  0.64 us (1%)
    pallas_call x1, Pallas kernels, shards(): pl.pallas_call(functools.partial(kernel, n_set, n_col), out_shape=(out, o...  49.4 us
    unnamed x2, local copies, waits for them, and re-layouts  3.34 us

profile of v2, /device:TPU:0, one launch (start us, length us, event | category | flops | bytes accessed | tf_op | source)
XLA Modules:
  0.0 53.4 jit_solution(14225098353574348282)
XLA Ops:
  0.6 49.4 %tomography_step.1 = (f32[8,64,128]{2,1,0:T(8,128)}, f32[8,64,128]{2,1,0:T(8,128)}) custom-call(s32[1,17]{1,0:T(1,128)} %labels.1, f32[2,2048,128]{2,1,0:T(8,128)} %bitcast.21, f32[8,64,128]{2,1,0:T(8,128)} %bitcast.23, s32[1024,128]{1,0:T(8,128)} %bitcast.22), custom_call_target="tpu_custom_call" | custom-call | tf_op jit(solution)/shard_map/tomography_step/pallas_call | solution.py:384
  50.1 1.7 %copy.12 = f32[8,2,4096]{2,1,0:T(2,128)} copy(f32[8,2,4096]{2,1,0:T(2,128)} %bitcast.25) | data formatting | bytes 524288
  51.7 1.7 %copy.13 = f32[8,2,4096]{2,1,0:T(2,128)} copy(f32[8,2,4096]{2,1,0:T(2,128)} %bitcast.24) | data formatting | bytes 524288

commit v3 on v2

--- a/solution.py
+++ b/solution.py
@@ -415,7 +415,7 @@
             dma((n_col, rank)), dma((n_col, rank)), dma((rank + 2,)),
         ],
         compiler_params=pltpu.CompilerParams(
-            collective_id=0, has_side_effects=True, vmem_limit_bytes=60 * 2**20),
+            collective_id=0, has_side_effects=True, vmem_limit_bytes=55888896),
         name="tomography_step",
     )(labels, interleave(factor), interleave(velocity), counts.reshape(order // LANES, LANES))
     return separate(new_factor), separate(new_velocity)

time: 53.6 us -> 51.4 us (0.959)
  local copies, waits for them, and re-layouts: 3.34 us -> 2.06 us
  Pallas kernels: 49.4 us -> 48.5 us
    unnamed x2 -> x4, local copies, waits for them, and re-layouts: 3.34 us -> 2.06 us
    pallas_call x1, Pallas kernels: 49.4 us -> 48.5 us  [shards(): pl.pallas_call(functools.partial(kernel, n_set, n_col), out_shape=(out, o...]
where the time goes in v3:
time: 51.4 us; the launch traced here: 51.2 us
  Pallas kernels  48.5 us (94%)
  local copies, waits for them, and re-layouts  2.06 us (4%)
  between operations  0.65 us (1%)
    pallas_call x1, Pallas kernels, shards(): pl.pallas_call(functools.partial(kernel, n_set, n_col), out_shape=(out, o...  48.5 us
    unnamed x4, local copies, waits for them, and re-layouts  2.06 us

profile of v3, /device:TPU:0, one launch (start us, length us, event | category | flops | bytes accessed | tf_op | source)
XLA Modules:
  0.0 51.2 jit_solution(3394597834342930504)
XLA Ops:
  0.6 0.0 copy-start
  0.6 0.6 %copy-done = s32[1,17]{1,0:T(1,128)S(1)} copy-done((s32[1,17]{1,0:T(1,128)S(1)}, s32[1,17]{1,0:T(1,128)}, u32[]{:S(2)}) %copy-start) | copy-done | bytes 92
  1.3 48.5 %tomography_step.1 = (f32[8,64,128]{2,1,0:T(8,128)S(1)}, f32[8,64,128]{2,1,0:T(8,128)S(1)}) custom-call(s32[1,17]{1,0:T(1,128)S(1)} %copy-done, f32[2,2048,128]{2,1,0:T(8,128)} %bitcast.23, f32[8,64,128]{2,1,0:T(8,128)} %bitcast.25, s32[1024,128]{1,0:T(8,128)} %bitcast.24), custom_call_target="tpu_custom_call" | custom-call | tf_op jit(solution)/shard_map/tomography_step/pallas_call | solution.py:384
  49.8 0.7 %copy.12 = f32[8,2,4096]{2,1,0:T(2,128)} copy(f32[8,2,4096]{2,1,0:T(2,128)S(1)} %bitcast.22) | data formatting | bytes 524288
  50.5 0.7 %copy.13 = f32[8,2,4096]{2,1,0:T(2,128)} copy(f32[8,2,4096]{2,1,0:T(2,128)S(1)} %bitcast.21) | data formatting | bytes 524288
Async XLA Ops:
  0.6 0.7 %copy-start = (s32[1,17]{1,0:T(1,128)S(1)}, s32[1,17]{1,0:T(1,128)}, u32[]{:S(2)}) copy-start(s32[1,17]{1,0:T(1,128)} %labels.1) | copy-start | bytes 208

commit v4 on v3

--- a/solution.py
+++ b/solution.py
@@ -151,6 +151,10 @@
             p_copies.append(copy(psend.at[s], precv.at[s], p_send.at[s], p_recv.at[s], (i, peer)))
             p_copies[-1].start()
 
+    loads[rank].wait()
+    count = jnp.concatenate(
+        [counts[pl.ds(j * (chunk * tiles) + b, chunk, stride=tiles), :] for b in range(tiles)], axis=1
+    ).astype(jnp.float32)
     prob = psend[0]
     for s, c in enumerate(p_copies, 1):
         c.wait()
@@ -158,10 +162,6 @@
     trace_value = prob[chunk : chunk + 1, :1]
     prob = prob[:chunk]
     quasi = (1.0 - mixing) * prob / trace_value + mixing / order
-    loads[rank].wait()
-    count = jnp.concatenate(
-        [counts[pl.ds(j * (chunk * tiles) + b, chunk, stride=tiles), :] for b in range(tiles)], axis=1
-    ).astype(jnp.float32)
     weight = count / (count_norm * order * quasi)
     wown[...] = weight
     w_copies = []
@@ -174,6 +174,7 @@
         folded = folded + ratio[:, b * LANES : (b + 1) * LANES]
     stat[:8, :] = folded
 
+    odd_late_mid = [phases(b) for b in range(tiles)]
     for s in range(n_col):
         if s:
             w_copies[s - 1].wait()
@@ -209,7 +210,6 @@
         return copy(y.at[r, rows_for(d, core)], left_buf.at[d, r], l_send.at[d, r], l_recv.at[d, r],
                     (lax.rem(i + n_set - 2, n_set), j))
 
-    odd_late_mid = [phases(b) for b in range(tiles)]
     for r in range(rank):
         re_all = dot(ha, high[2 * r]) + dot(ha, low[2 * r])
         im_all = dot(ha, high[2 * r + 1]) + dot(ha, low[2 * r + 1])

time: 51.4 us -> 51.4 us (level)
  no operation moved by 1% of the time
where the time goes in v4:
time: 51.4 us; the launch traced here: 51.2 us
  Pallas kernels  48.5 us (94%)
  local copies, waits for them, and re-layouts  2.06 us (4%)
  between operations  0.65 us (1%)
    pallas_call x1, Pallas kernels, shards(): pl.pallas_call(functools.partial(kernel, n_set, n_col), out_shape=(out, o...  48.5 us
    unnamed x4, local copies, waits for them, and re-layouts  2.06 us

profile of v4, /device:TPU:0, one launch (start us, length us, event | category | flops | bytes accessed | tf_op | source)
XLA Modules:
  0.0 51.2 jit_solution(221237308094856912)
XLA Ops:
  0.6 0.0 copy-start
  0.6 0.6 %copy-done = s32[1,17]{1,0:T(1,128)S(1)} copy-done((s32[1,17]{1,0:T(1,128)S(1)}, s32[1,17]{1,0:T(1,128)}, u32[]{:S(2)}) %copy-start) | copy-done | bytes 92
  1.3 48.5 %tomography_step.1 = (f32[8,64,128]{2,1,0:T(8,128)S(1)}, f32[8,64,128]{2,1,0:T(8,128)S(1)}) custom-call(s32[1,17]{1,0:T(1,128)S(1)} %copy-done, f32[2,2048,128]{2,1,0:T(8,128)} %bitcast.23, f32[8,64,128]{2,1,0:T(8,128)} %bitcast.25, s32[1024,128]{1,0:T(8,128)} %bitcast.24), custom_call_target="tpu_custom_call" | custom-call | tf_op jit(solution)/shard_map/tomography_step/pallas_call | solution.py:384
  49.8 0.7 %copy.12 = f32[8,2,4096]{2,1,0:T(2,128)} copy(f32[8,2,4096]{2,1,0:T(2,128)S(1)} %bitcast.22) | data formatting | bytes 524288
  50.5 0.7 %copy.13 = f32[8,2,4096]{2,1,0:T(2,128)} copy(f32[8,2,4096]{2,1,0:T(2,128)S(1)} %bitcast.21) | data formatting | bytes 524288
Async XLA Ops:
  0.6 0.7 %copy-start = (s32[1,17]{1,0:T(1,128)S(1)}, s32[1,17]{1,0:T(1,128)}, u32[]{:S(2)}) copy-start(s32[1,17]{1,0:T(1,128)} %labels.1) | copy-start | bytes 208
